TPU v7x, 512 devices: a whole 4x4x16 slice. The times are simulated.
512 devices in a mesh: blk: 64 (over z, x_hi, core), sub: 8 (over y, x_lo).
Axes of the slice: x: 4 (x_hi: 2, x_lo: 2; x = x_hi * 2 + x_lo), y: 4, z: 16, core: 2. Of those that a mesh axis runs over, the one named last changes fastest.
Arguments:
- features: float32 [12, 256, 8192], P(None, 'sub', 'blk'), may hold values from -6 to 6
- inverse_diag: float32 [6, 6, 256, 8192], P(None, None, 'sub', 'blk'), may hold values from -0.12 to 1, as said below
- couplings: float32 [4, 256, 8192], P(None, 'sub', 'blk'), may hold values from 0.2 to 0.24
- mismatch: float32 [6, 256, 8192], P(None, 'sub', 'blk'), may hold values from -21 to 21
- production: float32 [6, 256, 8192], P(None, 'sub', 'blk'), may hold values from -6 to 6
- weight_in: float32 [128, 12], replicated, may hold values from -1.75 to 1.75
- bias_in: float32 [128], replicated, may hold values from -0.5 to 0.5
- weight_two: float32 [128, 128], replicated, may hold values from -0.5 to 0.5
- bias_two: float32 [128], replicated, may hold values from -0.5 to 0.5
- weight_three: float32 [128, 128], replicated, may hold values from -0.5 to 0.5
- bias_three: float32 [128], replicated, may hold values from -0.5 to 0.5
- weight_four: float32 [128, 128], replicated, may hold values from -0.5 to 0.5
- bias_four: float32 [128], replicated, may hold values from -0.5 to 0.5
- weight_out: float32 [128], replicated, may hold values from -0.5 to 0.5
Outputs:
- adjoint: float32 [6, 256, 8192], P(None, 'sub', 'blk')
- sensitivity: float32 [256, 8192], P('sub', 'blk')
- correction: float32 [256, 8192], P('sub', 'blk')
- grad_weight_in: float32 [128, 12], replicated
- grad_bias_in: float32 [128], replicated
- grad_weight_two: float32 [128, 128], replicated
- grad_bias_two: float32 [128], replicated
- grad_weight_three: float32 [128, 128], replicated
- grad_bias_three: float32 [128], replicated
- grad_weight_four: float32 [128, 128], replicated
- grad_bias_four: float32 [128], replicated
- grad_weight_out: float32 [128], replicated
Inputs may be any that keep to these rules, and one draw needn't show every extreme that they name: `inverse_diag`: a cell's 6 by 6 block with diagonal entries between 0.7 and 1.0 and off-diagonal entries of magnitude at most 0.12.
All inputs are finite; a program needn't handle non-finite values.
Results may differ from a plain program's by a relative error of at most 0.0003.
Values sent between devices are 32-bit elements; how exact they have to be, the bound alone decides.
No kernel may reach another device: no remote copies, remote signals or barrier semaphores. Data moves between devices by JAX's collectives and lax.ppermute only.
A program may use at most 64 MiB of HBM per device.

v0:
```python
import jax
import jax.numpy as jnp
from jax import lax
from jax.sharding import PartitionSpec as P

SWEEPS = 8
EPS = 1e-06
HIGH = lax.Precision.HIGHEST


def padded_2(value, sides, width, wrap):
    for axis, dim in sides:
        devices, length = (lax.axis_size(axis), value.shape[dim])
        up = [(i, (i + 1) % devices) for i in range(devices if wrap else devices - 1)]
        down = [(j, i) for i, j in up]
        last = lax.slice_in_dim(value, length - width, length, axis=dim)
        initial = lax.slice_in_dim(value, 0, width, axis=dim)
        before = lax.ppermute(last, axis, up)
        after = lax.ppermute(initial, axis, down)
        value = jnp.concatenate([before, value, after], axis=dim)
    return value


def sweep_padded(padded, inverse_diag, couplings, mismatch):
    upper_side = padded[:, :-2, 1:-1]
    lower_side = padded[:, 2:, 1:-1]
    pitch_low = padded[:, 1:-1, :-2]
    pitch_high = padded[:, 1:-1, 2:]
    rhs = mismatch + couplings[0] * upper_side + couplings[1] * lower_side
    rhs = rhs + couplings[2] * pitch_low + couplings[3] * pitch_high
    return jnp.sum(inverse_diag * rhs[None], axis=1)


def forward(inputs, weights):
    weight_in, bias_in, weight_two, bias_two, weight_three, bias_three, weight_four, bias_four = (
        weights
    )
    layer_one = jnp.tanh(
        jnp.einsum("ij,jc->ic", weight_in, inputs, precision=HIGH) + bias_in[:, None]
    )
    layer_two = jnp.tanh(
        jnp.einsum("ij,jc->ic", weight_two, layer_one, precision=HIGH) + bias_two[:, None]
    )
    layer_three = jnp.tanh(
        jnp.einsum("ij,jc->ic", weight_three, layer_two, precision=HIGH) + bias_three[:, None]
    )
    layer_four = jnp.tanh(
        jnp.einsum("ij,jc->ic", weight_four, layer_three, precision=HIGH) + bias_four[:, None]
    )
    return (layer_one, layer_two, layer_three, layer_four)


def top_terms(layer_four, layer_three, upstream, weight_out):
    grad_out = jnp.einsum("ic,c->i", layer_four, upstream, precision=HIGH)
    delta_four = weight_out[:, None] * upstream[None, :] * (1.0 - layer_four * layer_four)
    grad_four = jnp.einsum("ic,jc->ij", delta_four, layer_three, precision=HIGH)
    return (grad_out, grad_four, jnp.sum(delta_four, axis=1), delta_four)


def next_terms(delta_next, weight_next, layer_now, layer_prev):
    delta_now = jnp.einsum("ji,jc->ic", weight_next, delta_next, precision=HIGH) * (
        1.0 - layer_now * layer_now
    )
    grad_now = jnp.einsum("ic,jc->ij", delta_now, layer_prev, precision=HIGH)
    return (grad_now, jnp.sum(delta_now, axis=1), delta_now)


def local(
    features,
    inverse_diag,
    couplings,
    mismatch,
    production,
    weight_in,
    bias_in,
    weight_two,
    bias_two,
    weight_three,
    bias_three,
    weight_four,
    bias_four,
    weight_out,
):
    nvars, rows, cols = mismatch.shape
    adjoint = jnp.zeros((nvars, rows, cols), jnp.float32)
    for sweep_index in range(SWEEPS):
        widened = padded_2(adjoint, (("blk", 2),), 1, True)
        padded = padded_2(widened, (("sub", 1),), 1, False)
        adjoint = sweep_padded(padded, inverse_diag, couplings, mismatch)
    sensitivity = -jnp.sum(adjoint * production, axis=0)
    local_square = jnp.sum(sensitivity * sensitivity)
    inputs = features.reshape(features.shape[0], rows * cols)
    weights = (
        weight_in,
        bias_in,
        weight_two,
        bias_two,
        weight_three,
        bias_three,
        weight_four,
        bias_four,
    )
    layer_one, layer_two, layer_three, layer_four = forward(inputs, weights)
    correction = (1.0 + jnp.einsum("i,ic->c", weight_out, layer_four, precision=HIGH)).reshape(
        rows, cols
    )
    flat_sens = sensitivity.reshape(rows * cols)
    total_square = lax.psum(local_square, ("blk", "sub"))
    norm_value = jnp.sqrt(total_square + EPS)
    upstream = flat_sens / norm_value
    grad_out, grad_four, gb_four, delta_four = top_terms(
        layer_four, layer_three, upstream, weight_out
    )
    grad_out, grad_four, gb_four = lax.psum((grad_out, grad_four, gb_four), ("blk", "sub"))
    grad_three, gb_three, delta_three = next_terms(delta_four, weight_four, layer_three, layer_two)
    grad_three, gb_three = lax.psum((grad_three, gb_three), ("blk", "sub"))
    grad_two, gb_two, delta_two = next_terms(delta_three, weight_three, layer_two, layer_one)
    grad_two, gb_two = lax.psum((grad_two, gb_two), ("blk", "sub"))
    grad_one, gb_one, delta_one = next_terms(delta_two, weight_two, layer_one, inputs)
    grad_one, gb_one = lax.psum((grad_one, gb_one), ("blk", "sub"))
    results = (
        grad_one,
        gb_one,
        grad_two,
        gb_two,
        grad_three,
        gb_three,
        grad_four,
        gb_four,
        grad_out,
    )
    return (
        adjoint,
        sensitivity,
        correction,
        results[0],
        results[1],
        results[2],
        results[3],
        results[4],
        results[5],
        results[6],
        results[7],
        results[8],
    )


def solution(mesh):
    placed = (
        P(None, "sub", "blk"),
        P(None, None, "sub", "blk"),
        P(None, "sub", "blk"),
        P(None, "sub", "blk"),
        P(None, "sub", "blk"),
        P(),
        P(),
        P(),
        P(),
        P(),
        P(),
        P(),
        P(),
        P(),
    )
    return jax.shard_map(
        local,
        mesh=mesh,
        in_specs=placed,
        out_specs=(
            P(None, "sub", "blk"),
            P("sub", "blk"),
            P("sub", "blk"),
            P(),
            P(),
            P(),
            P(),
            P(),
            P(),
            P(),
            P(),
            P(),
        ),
        check_vma=False,
    )
```

profile of v0, /device:TPU:1, one launch (start us, length us, event | category | flops | bytes accessed | tf_op | source)
XLA Modules:
  0.0 789.4 jit_solution(17911993634000659095)
XLA Ops:
  7.3 8.9 %collective-permute-start.1 = (f32[6,32,1]{2,1,0:T(8,128)S(1)}, f32[6,32,1]{2,1,0:T(8,128)S(1)}, u32[]{:S(2)}, u32[]{:S(2)}) collective-permute-start(f32[6,32,1]{2,1,0:T(8,128)S(1)} %broadcast.37), channel_id=1, source_target_pairs={{8,0},{16,8},{24,16},{32,24},{40,32},{48,40},{56,48},{64,56},{72,6... | collective-permute-start | bytes 2312 | tf_op jit(solution)/shard_map/ppermute | solution.py:19
  18.1 6.8 collective-permute-done
  36.6 9.9 %collective-permute-start.5 = (f32[6,32,1]{2,1,0:T(8,128)S(1)}, f32[6,32,1]{2,1,0:T(8,128)S(1)}, u32[]{:S(2)}, u32[]{:S(2)}) collective-permute-start(f32[6,32,1]{2,1,0:T(8,128)S(1)} %get-tuple-element.52), channel_id=1, source_target_pairs={{8,0},{16,8},{24,16},{32,24},{40,32},{48,40},{56,48},{64,56},{72,6... | collective-permute-start | bytes 2312 | tf_op jit(solution)/shard_map/ppermute | solution.py:19
  47.5 4.5 collective-permute-start.6
  58.8 10.0 %collective-permute-start.9 = (f32[6,32,1]{2,1,0:T(8,128)S(1)}, f32[6,32,1]{2,1,0:T(8,128)S(1)}, u32[]{:S(2)}, u32[]{:S(2)}) collective-permute-start(f32[6,32,1]{2,1,0:T(8,128)S(1)} %get-tuple-element.50), channel_id=1, source_target_pairs={{8,0},{16,8},{24,16},{32,24},{40,32},{48,40},{56,48},{64,56},{72,6... | collective-permute-start | bytes 2312 | tf_op jit(solution)/shard_map/ppermute | solution.py:19
  73.7 3.3 collective-permute-done.11
  79.4 9.7 %collective-permute-start.13 = (f32[6,32,1]{2,1,0:T(8,128)S(1)}, f32[6,32,1]{2,1,0:T(8,128)S(1)}, u32[]{:S(2)}, u32[]{:S(2)}) collective-permute-start(f32[6,32,1]{2,1,0:T(8,128)S(1)} %get-tuple-element.48), channel_id=1, source_target_pairs={{8,0},{16,8},{24,16},{32,24},{40,32},{48,40},{56,48},{64,56},{72,6... | collective-permute-start | bytes 2312 | tf_op jit(solution)/shard_map/ppermute | solution.py:19
  90.1 4.5 collective-permute-start.14
  101.3 10.0 %collective-permute-start.17 = (f32[6,32,1]{2,1,0:T(8,128)S(1)}, f32[6,32,1]{2,1,0:T(8,128)S(1)}, u32[]{:S(2)}, u32[]{:S(2)}) collective-permute-start(f32[6,32,1]{2,1,0:T(8,128)S(1)} %get-tuple-element.46), channel_id=1, source_target_pairs={{8,0},{16,8},{24,16},{32,24},{40,32},{48,40},{56,48},{64,56},{72,6... | collective-permute-start | bytes 2312 | tf_op jit(solution)/shard_map/ppermute | solution.py:19
  116.3 3.2 collective-permute-done.19
  121.8 10.0 %collective-permute-start.21 = (f32[6,32,1]{2,1,0:T(8,128)S(1)}, f32[6,32,1]{2,1,0:T(8,128)S(1)}, u32[]{:S(2)}, u32[]{:S(2)}) collective-permute-start(f32[6,32,1]{2,1,0:T(8,128)S(1)} %get-tuple-element.44), channel_id=1, source_target_pairs={{8,0},{16,8},{24,16},{32,24},{40,32},{48,40},{56,48},{64,56},{72,6... | collective-permute-start | bytes 2312 | tf_op jit(solution)/shard_map/ppermute | solution.py:19
  132.8 4.2 collective-permute-start.22
  143.7 10.0 %collective-permute-start.25 = (f32[6,32,1]{2,1,0:T(8,128)S(1)}, f32[6,32,1]{2,1,0:T(8,128)S(1)}, u32[]{:S(2)}, u32[]{:S(2)}) collective-permute-start(f32[6,32,1]{2,1,0:T(8,128)S(1)} %get-tuple-element.42), channel_id=1, source_target_pairs={{8,0},{16,8},{24,16},{32,24},{40,32},{48,40},{56,48},{64,56},{72,6... | collective-permute-start | bytes 2312 | tf_op jit(solution)/shard_map/ppermute | solution.py:19
  164.2 10.0 %collective-permute-start.29 = (f32[6,32,1]{2,1,0:T(8,128)S(1)}, f32[6,32,1]{2,1,0:T(8,128)S(1)}, u32[]{:S(2)}, u32[]{:S(2)}) collective-permute-start(f32[6,32,1]{2,1,0:T(8,128)S(1)} %get-tuple-element.40), channel_id=1, source_target_pairs={{8,0},{16,8},{24,16},{32,24},{40,32},{48,40},{56,48},{64,56},{72,6... | collective-permute-start | bytes 2312 | tf_op jit(solution)/shard_map/ppermute | solution.py:19
  180.7 3.4 fusion.4
  185.5 3.2 fusion.3
  188.7 108.6 %psum.70 = f32[]{:T(128)} all-reduce(f32[]{:T(128)} %multiply_reduce_fusion.9), channel_id=1, replica_groups=mesh['blk'=64,'sub'=8] {'blk','sub'}, use_global_device_ids=true, to_apply=%region_10.0 | all-reduce | flops 1 | bytes 8 | tf_op jit(solution)/shard_map/psum | solution.py:108
  298.6 4.0 fusion.6
  307.4 3.6 fusion.91
  311.0 4.4 fusion.94
  318.6 4.2 fusion.93
  322.8 4.5 fusion.89
  331.4 99.6 %all-reduce.2 = (f32[128,12]{0,1:T(8,128)}, f32[128]{0:T(128)}, f32[128]{0:T(128)}, f32[128]{0:T(128)}, f32[128]{0:T(128)}, /*index=5*/f32[128]{0:T(128)}) all-reduce(f32[128,12]{0,1:T(8,128)S(1)} %fusion.92, f32[128]{0:T(128)S(1)} %get-tuple-element.57, ...), channel_id=1, replica_groups=mesh['blk'=64,'sub'=8] {'blk','sub'}, use_global_device_ids=true, to_apply=%region_11.0 | all-reduce | flops 2176 | bytes 17408 | tf_op jit(solution)/shard_map/psum | solution.py:120
  431.1 346.9 %all-reduce.6.cloned.1.call-done = (f32[128,128]{1,0:T(8,128)}, f32[128,128]{1,0:T(8,128)}, f32[128,128]{1,0:T(8,128)}) async-done(((f32[128,128]{1,0:T(8,128)}, f32[128,128]{1,0:T(8,128)}, f32[128,128]{1,0:T(8,128)}), (f32[128,128]{1,0:T(8,128)}, f32[128,128]{1,0:T(8,128)}, f32[128,128]{1,0:T(8,128)})) %all-reduce.6.cloned.1.call-update) | async-done | bytes 196624 | tf_op jit(solution)/shard_map/psum | solution.py:118
  (141 shorter events, 86.3 us)
Async XLA Ops:
  7.2 770.7 %all-reduce.6.cloned.1.call-start = ((), (), s32[]{:S(2)}) async-start(), calls=%async_computation | async-start | bytes 393216 | tf_op jit(solution)/shard_map/psum | solution.py:118
  7.3 10.9 %collective-permute-start.1 = (f32[6,32,1]{2,1,0:T(8,128)S(1)}, f32[6,32,1]{2,1,0:T(8,128)S(1)}, u32[]{:S(2)}, u32[]{:S(2)}) collective-permute-start(f32[6,32,1]{2,1,0:T(8,128)S(1)} %broadcast.37), channel_id=1, source_target_pairs={{8,0},{16,8},{24,16},{32,24},{40,32},{48,40},{56,48},{64,56},{72,6... | collective-permute-start | bytes 2312 | tf_op jit(solution)/shard_map/ppermute | solution.py:19
  16.2 8.7 %collective-permute-start = (f32[6,32,1]{2,1,0:T(8,128)S(1)}, f32[6,32,1]{2,1,0:T(8,128)S(1)}, u32[]{:S(2)}, u32[]{:S(2)}) collective-permute-start(f32[6,32,1]{2,1,0:T(8,128)S(1)} %broadcast.37), channel_id=1, source_target_pairs={{0,8},{8,16},{16,24},{24,32},{32,40},{40,48},{48,56},{56,64},{64,7... | collective-permute-start | bytes 2312 | tf_op jit(solution)/shard_map/ppermute | solution.py:18
  27.3 5.1 collective-permute-start.3
  34.7 11.8 %collective-permute-start.4 = (f32[6,32,1]{2,1,0:T(8,128)S(1)}, f32[6,32,1]{2,1,0:T(8,128)S(1)}, u32[]{:S(2)}, u32[]{:S(2)}) collective-permute-start(f32[6,32,1]{2,1,0:T(8,128)S(1)} %get-tuple-element.51), channel_id=1, source_target_pairs={{0,8},{8,16},{16,24},{24,32},{32,40},{40,48},{48,56},{56,64},{64,7... | collective-permute-start | bytes 2312 | tf_op jit(solution)/shard_map/ppermute | solution.py:18
  36.6 10.8 %collective-permute-start.5 = (f32[6,32,1]{2,1,0:T(8,128)S(1)}, f32[6,32,1]{2,1,0:T(8,128)S(1)}, u32[]{:S(2)}, u32[]{:S(2)}) collective-permute-start(f32[6,32,1]{2,1,0:T(8,128)S(1)} %get-tuple-element.52), channel_id=1, source_target_pairs={{8,0},{16,8},{24,16},{32,24},{40,32},{48,40},{56,48},{64,56},{72,6... | collective-permute-start | bytes 2312 | tf_op jit(solution)/shard_map/ppermute | solution.py:19
  47.5 5.8 collective-permute-start.6
  56.8 11.9 %collective-permute-start.8 = (f32[6,32,1]{2,1,0:T(8,128)S(1)}, f32[6,32,1]{2,1,0:T(8,128)S(1)}, u32[]{:S(2)}, u32[]{:S(2)}) collective-permute-start(f32[6,32,1]{2,1,0:T(8,128)S(1)} %get-tuple-element.49), channel_id=1, source_target_pairs={{0,8},{8,16},{16,24},{24,32},{32,40},{40,48},{48,56},{56,64},{64,7... | collective-permute-start | bytes 2312 | tf_op jit(solution)/shard_map/ppermute | solution.py:18
  58.8 10.9 %collective-permute-start.9 = (f32[6,32,1]{2,1,0:T(8,128)S(1)}, f32[6,32,1]{2,1,0:T(8,128)S(1)}, u32[]{:S(2)}, u32[]{:S(2)}) collective-permute-start(f32[6,32,1]{2,1,0:T(8,128)S(1)} %get-tuple-element.50), channel_id=1, source_target_pairs={{8,0},{16,8},{24,16},{32,24},{40,32},{48,40},{56,48},{64,56},{72,6... | collective-permute-start | bytes 2312 | tf_op jit(solution)/shard_map/ppermute | solution.py:19
  72.4 4.7 collective-permute-start.11
  77.4 11.6 %collective-permute-start.12 = (f32[6,32,1]{2,1,0:T(8,128)S(1)}, f32[6,32,1]{2,1,0:T(8,128)S(1)}, u32[]{:S(2)}, u32[]{:S(2)}) collective-permute-start(f32[6,32,1]{2,1,0:T(8,128)S(1)} %get-tuple-element.47), channel_id=1, source_target_pairs={{0,8},{8,16},{16,24},{24,32},{32,40},{40,48},{48,56},{56,64},{64,7... | collective-permute-start | bytes 2312 | tf_op jit(solution)/shard_map/ppermute | solution.py:18
  79.4 10.6 %collective-permute-start.13 = (f32[6,32,1]{2,1,0:T(8,128)S(1)}, f32[6,32,1]{2,1,0:T(8,128)S(1)}, u32[]{:S(2)}, u32[]{:S(2)}) collective-permute-start(f32[6,32,1]{2,1,0:T(8,128)S(1)} %get-tuple-element.48), channel_id=1, source_target_pairs={{8,0},{16,8},{24,16},{32,24},{40,32},{48,40},{56,48},{64,56},{72,6... | collective-permute-start | bytes 2312 | tf_op jit(solution)/shard_map/ppermute | solution.py:19
  90.1 5.8 collective-permute-start.14
  99.4 11.9 %collective-permute-start.16 = (f32[6,32,1]{2,1,0:T(8,128)S(1)}, f32[6,32,1]{2,1,0:T(8,128)S(1)}, u32[]{:S(2)}, u32[]{:S(2)}) collective-permute-start(f32[6,32,1]{2,1,0:T(8,128)S(1)} %get-tuple-element.45), channel_id=1, source_target_pairs={{0,8},{8,16},{16,24},{24,32},{32,40},{40,48},{48,56},{56,64},{64,7... | collective-permute-start | bytes 2312 | tf_op jit(solution)/shard_map/ppermute | solution.py:18
  101.3 10.9 %collective-permute-start.17 = (f32[6,32,1]{2,1,0:T(8,128)S(1)}, f32[6,32,1]{2,1,0:T(8,128)S(1)}, u32[]{:S(2)}, u32[]{:S(2)}) collective-permute-start(f32[6,32,1]{2,1,0:T(8,128)S(1)} %get-tuple-element.46), channel_id=1, source_target_pairs={{8,0},{16,8},{24,16},{32,24},{40,32},{48,40},{56,48},{64,56},{72,6... | collective-permute-start | bytes 2312 | tf_op jit(solution)/shard_map/ppermute | solution.py:19
  119.8 11.9 %collective-permute-start.20 = (f32[6,32,1]{2,1,0:T(8,128)S(1)}, f32[6,32,1]{2,1,0:T(8,128)S(1)}, u32[]{:S(2)}, u32[]{:S(2)}) collective-permute-start(f32[6,32,1]{2,1,0:T(8,128)S(1)} %get-tuple-element.43), channel_id=1, source_target_pairs={{0,8},{8,16},{16,24},{24,32},{32,40},{40,48},{48,56},{56,64},{64,7... | collective-permute-start | bytes 2312 | tf_op jit(solution)/shard_map/ppermute | solution.py:18
  121.8 10.9 %collective-permute-start.21 = (f32[6,32,1]{2,1,0:T(8,128)S(1)}, f32[6,32,1]{2,1,0:T(8,128)S(1)}, u32[]{:S(2)}, u32[]{:S(2)}) collective-permute-start(f32[6,32,1]{2,1,0:T(8,128)S(1)} %get-tuple-element.44), channel_id=1, source_target_pairs={{8,0},{16,8},{24,16},{32,24},{40,32},{48,40},{56,48},{64,56},{72,6... | collective-permute-start | bytes 2312 | tf_op jit(solution)/shard_map/ppermute | solution.py:19
  132.8 5.5 collective-permute-start.22
  141.8 11.9 %collective-permute-start.24 = (f32[6,32,1]{2,1,0:T(8,128)S(1)}, f32[6,32,1]{2,1,0:T(8,128)S(1)}, u32[]{:S(2)}, u32[]{:S(2)}) collective-permute-start(f32[6,32,1]{2,1,0:T(8,128)S(1)} %get-tuple-element.41), channel_id=1, source_target_pairs={{0,8},{8,16},{16,24},{24,32},{32,40},{40,48},{48,56},{56,64},{64,7... | collective-permute-start | bytes 2312 | tf_op jit(solution)/shard_map/ppermute | solution.py:18
  143.7 10.9 %collective-permute-start.25 = (f32[6,32,1]{2,1,0:T(8,128)S(1)}, f32[6,32,1]{2,1,0:T(8,128)S(1)}, u32[]{:S(2)}, u32[]{:S(2)}) collective-permute-start(f32[6,32,1]{2,1,0:T(8,128)S(1)} %get-tuple-element.42), channel_id=1, source_target_pairs={{8,0},{16,8},{24,16},{32,24},{40,32},{48,40},{56,48},{64,56},{72,6... | collective-permute-start | bytes 2312 | tf_op jit(solution)/shard_map/ppermute | solution.py:19
  162.3 13.8 %collective-permute-start.28 = (f32[6,32,1]{2,1,0:T(8,128)S(1)}, f32[6,32,1]{2,1,0:T(8,128)S(1)}, u32[]{:S(2)}, u32[]{:S(2)}) collective-permute-start(f32[6,32,1]{2,1,0:T(8,128)S(1)} %get-tuple-element.39), channel_id=1, source_target_pairs={{0,8},{8,16},{16,24},{24,32},{32,40},{40,48},{48,56},{56,64},{64,7... | collective-permute-start | bytes 2312 | tf_op jit(solution)/shard_map/ppermute | solution.py:18
  164.2 11.9 %collective-permute-start.29 = (f32[6,32,1]{2,1,0:T(8,128)S(1)}, f32[6,32,1]{2,1,0:T(8,128)S(1)}, u32[]{:S(2)}, u32[]{:S(2)}) collective-permute-start(f32[6,32,1]{2,1,0:T(8,128)S(1)} %get-tuple-element.40), channel_id=1, source_target_pairs={{8,0},{16,8},{24,16},{32,24},{40,32},{48,40},{56,48},{64,56},{72,6... | collective-permute-start | bytes 2312 | tf_op jit(solution)/shard_map/ppermute | solution.py:19
  176.2 8.0 %collective-permute-start.30 = (f32[6,1,130]{2,1,0:T(1,128)S(1)}, f32[6,1,130]{2,1,0:T(1,128)S(1)}, u32[]{:S(2)}, u32[]{:S(2)}) collective-permute-start(f32[6,1,130]{2,1,0:T(1,128)S(1)} %get-tuple-element.23), channel_id=1, source_target_pairs={{0,1},{1,2},{2,3},{3,4},{4,5},{5,6},{6,7},{8,9},{9,10},{10,11},{11... | collective-permute-start | bytes 9368 | tf_op jit(solution)/shard_map/ppermute | solution.py:18
  178.8 5.4 collective-permute-start.31
  (29 other events, 852.5 us)
Sparse Core Ops, SparseCore 0:
  329.8 448.0 all-reduce.5
where the time goes:
time: 796 us; the launch traced here: 789 us
  waiting for transfers between devices  381 us (48%)
  blocking collectives  208 us (26%)
  starting transfers between devices  131 us (16%)
  matrix products  38.9 us (5%)
  between operations  15.8 us (2%)
    psum x1, waiting for transfers between devices, local(): grad_two, gb_two = lax.psum((grad_two, gb_two), ('blk', 'sub'))  347 us
    psum x1, blocking collectives, local(): total_square = lax.psum(local_square, ('blk', 'sub'))  109 us
    psum x1, blocking collectives, local(): grad_one, gb_one = lax.psum((grad_one, gb_one), ('blk', 'sub'))  99.6 us
    ppermute x16, starting transfers between devices, padded_2(): after = lax.ppermute(initial, axis, down)  89.2 us
    ppermute x16, starting transfers between devices, padded_2(): before = lax.ppermute(last, axis, up)  41.6 us
    ppermute x16, waiting for transfers between devices, padded_2(): after = lax.ppermute(initial, axis, down)  27 us
  transfers between devices with their start and end apart: 33, of which 15 were waited for; matrix products, arithmetic and copies ran while one was open for 1% of the time, Pallas kernels for 0%

commit v1 on v0

--- a/solution.py
+++ b/solution.py
@@ -115,7 +115,7 @@
     grad_three, gb_three, delta_three = next_terms(delta_four, weight_four, layer_three, layer_two)
     grad_three, gb_three = lax.psum((grad_three, gb_three), ("blk", "sub"))
     grad_two, gb_two, delta_two = next_terms(delta_three, weight_three, layer_two, layer_one)
-    grad_two, gb_two = lax.psum((grad_two, gb_two), ("blk", "sub"))
+    grad_two, gb_two = lax.psum(lax.psum((grad_two, gb_two), "sub"), "blk")
     grad_one, gb_one, delta_one = next_terms(delta_two, weight_two, layer_one, inputs)
     grad_one, gb_one = lax.psum((grad_one, gb_one), ("blk", "sub"))
     results = (

time: 796 us -> 1330 us (1.67)
  waiting for transfers between devices: 381 us -> 758 us
  blocking collectives: 208 us -> 361 us
    psum x1 -> x3, waiting for transfers between devices: 347 us -> 724 us  [the longest x2 518 us: local(): grad_two, gb_two = lax.psum(lax.psum((grad_two, gb_two), 'sub'), 'blk')]
    psum x0 -> x2, blocking collectives: none -> 153 us  [local(): grad_two, gb_two = lax.psum(lax.psum((grad_two, gb_two), 'sub'), 'blk')]
  transfers between devices with their start and end apart: 33 -> 35, of which waited for: 15 -> 17; matrix products, arithmetic and copies ran while one was open for 1% -> 1% of each run, Pallas kernels for 0% -> 0%
where the time goes in v1:
time: 1330 us; the launch traced here: 1320 us
  waiting for transfers between devices  758 us (57%)
  blocking collectives  361 us (27%)
  starting transfers between devices  131 us (10%)
  matrix products  41.5 us (3%)
  between operations  15.5 us (1%)
    psum x2, waiting for transfers between devices, local(): grad_two, gb_two = lax.psum(lax.psum((grad_two, gb_two), 'sub'), 'blk')  518 us
    psum x1, waiting for transfers between devices, local(): grad_three, gb_three = lax.psum((grad_three, gb_three), ('blk', 'sub'))  206 us
    psum x2, blocking collectives, local(): grad_two, gb_two = lax.psum(lax.psum((grad_two, gb_two), 'sub'), 'blk')  153 us
    psum x1, blocking collectives, local(): total_square = lax.psum(local_square, ('blk', 'sub'))  109 us
    psum x1, blocking collectives, local(): grad_one, gb_one = lax.psum((grad_one, gb_one), ('blk', 'sub'))  99.8 us
    ppermute x16, starting transfers between devices, padded_2(): after = lax.ppermute(initial, axis, down)  89.2 us
    ppermute x16, starting transfers between devices, padded_2(): before = lax.ppermute(last, axis, up)  41.6 us
    ppermute x16, waiting for transfers between devices, padded_2(): after = lax.ppermute(initial, axis, down)  27 us
  transfers between devices with their start and end apart: 35, of which 17 were waited for; matrix products, arithmetic and copies ran while one was open for 1% of the time, Pallas kernels for 0%

profile of v1, /device:TPU:1, one launch (start us, length us, event | category | flops | bytes accessed | tf_op | source)
XLA Modules:
  0.0 1322.6 jit_solution(10811605270323177331)
XLA Ops:
  7.3 8.9 collective-permute-start.1
  18.1 6.8 collective-permute-done
  36.6 9.9 collective-permute-start.5
  47.5 4.5 collective-permute-start.6
  58.8 10.0 collective-permute-start.9
  79.4 9.7 collective-permute-start.13
  90.1 4.5 collective-permute-start.14
  101.3 10.0 collective-permute-start.17
  121.8 10.0 collective-permute-start.21
  132.8 4.2 collective-permute-start.22
  143.7 10.0 collective-permute-start.25
  164.2 10.0 collective-permute-start.29
  188.7 108.6 %psum.84 = f32[]{:T(128)} all-reduce(f32[]{:T(128)} %multiply_reduce_fusion.9), channel_id=1, replica_groups=mesh['blk'=64,'sub'=8] {'blk','sub'}, use_global_device_ids=true, to_apply=%region_10.0 | all-reduce | flops 1 | bytes 8 | tf_op jit(solution)/shard_map/psum | solution.py:108
  298.6 4.2 fusion.6
  310.9 4.4 fusion.94
  315.3 4.3 fusion.91
  320.9 4.2 fusion.93
  325.1 4.5 fusion.89
  333.3 73.4 %all-reduce.8.cloned.1.call-done = f32[128,128]{1,0:T(8,128)} async-done(((f32[128,128]{1,0:T(8,128)}), f32[128,128]{1,0:T(8,128)}) %all-reduce.8.cloned.1.call-update) | async-done | bytes 65552 | tf_op jit(solution)/shard_map/psum | solution.py:118
  408.5 14.0 %psum.89 = f32[128]{0:T(128)S(1)} all-reduce(f32[128]{0:T(128)S(1)} %get-tuple-element.61), channel_id=1, replica_groups=mesh['blk'=64,'sub'=8] {'sub'}, use_global_device_ids=true, to_apply=%region_17.0 | all-reduce | flops 128 | bytes 1024 | tf_op jit(solution)/shard_map/psum | solution.py:118
  422.5 138.7 %psum.90 = f32[128]{0:T(128)} all-reduce(f32[128]{0:T(128)S(1)} %psum.89), channel_id=1, replica_groups=mesh['blk'=64,'sub'=8] {'blk'}, use_global_device_ids=true, to_apply=%region_18.0 | all-reduce | flops 128 | bytes 1024 | tf_op jit(solution)/shard_map/psum | solution.py:118
  561.1 99.8 %all-reduce.2 = (f32[128,12]{0,1:T(8,128)}, f32[128]{0:T(128)}, f32[128]{0:T(128)}, f32[128]{0:T(128)}, f32[128]{0:T(128)}) all-reduce(f32[128,12]{0,1:T(8,128)S(1)} %fusion.92, f32[128]{0:T(128)S(1)} %get-tuple-element.55, f32[128]{0:T(128)S(1)} %get-tuple-element.57, ...), channel_id=1, replica_groups=mesh['blk'=64,'sub'=8] {'blk','sub'}, use_global_device_ids=true, to_apply=%region_11.0 | all-reduce | flops 2048 | bytes 16384 | tf_op jit(solution)/shard_map/psum | solution.py:120
  661.0 206.2 %all-reduce.12.cloned.1.call-done = (f32[128,128]{1,0:T(8,128)}, f32[128,128]{1,0:T(8,128)}) async-done(((f32[128,128]{1,0:T(8,128)}, f32[128,128]{1,0:T(8,128)}), (f32[128,128]{1,0:T(8,128)}, f32[128,128]{1,0:T(8,128)})) %all-reduce.12.cloned.1.call-update) | async-done | bytes 131088 | tf_op jit(solution)/shard_map/psum | solution.py:116
  867.2 444.2 %all-reduce.10.cloned.1.call-done = f32[128,128]{1,0:T(8,128)} async-done(((f32[128,128]{1,0:T(8,128)}), f32[128,128]{1,0:T(8,128)}) %all-reduce.10.cloned.1.call-update) | async-done | bytes 65552 | tf_op jit(solution)/shard_map/psum | solution.py:118
  (151 shorter events, 102.1 us)
Async XLA Ops:
  7.2 399.5 %all-reduce.8.cloned.1.call-start = ((), (), s32[]{:S(2)}) async-start(), calls=%async_computation | async-start | bytes 131072 | tf_op jit(solution)/shard_map/psum | solution.py:118
  7.3 10.9 collective-permute-start.1
  16.2 8.7 collective-permute-start
  34.6 11.8 collective-permute-start.4
  36.6 10.8 collective-permute-start.5
  47.5 5.8 collective-permute-start.6
  56.8 11.9 collective-permute-start.8
  58.8 10.9 collective-permute-start.9
  77.4 11.6 collective-permute-start.12
  79.4 10.6 collective-permute-start.13
  90.1 5.8 collective-permute-start.14
  99.4 11.9 collective-permute-start.16
  101.3 10.9 collective-permute-start.17
  119.8 11.9 collective-permute-start.20
  121.8 10.9 collective-permute-start.21
  132.8 5.5 collective-permute-start.22
  141.8 11.9 collective-permute-start.24
  143.7 10.9 collective-permute-start.25
  162.3 13.8 %collective-permute-start.28 = (f32[6,32,1]{2,1,0:T(8,128)S(1)}, f32[6,32,1]{2,1,0:T(8,128)S(1)}, u32[]{:S(2)}, u32[]{:S(2)}) collective-permute-start(f32[6,32,1]{2,1,0:T(8,128)S(1)} %get-tuple-element.37), channel_id=1, source_target_pairs={{0,8},{8,16},{16,24},{24,32},{32,40},{40,48},{48,56},{56,64},{64,7... | collective-permute-start | bytes 2312 | tf_op jit(solution)/shard_map/ppermute | solution.py:18
  164.2 11.9 collective-permute-start.29
  176.2 8.0 collective-permute-start.30
  178.8 5.4 collective-permute-start.31
  331.4 535.8 %all-reduce.12.cloned.1.call-start = ((), (), s32[]{:S(2)}) async-start(), calls=%async_computation.2 | async-start | bytes 262144 | tf_op jit(solution)/shard_map/psum | solution.py:116
  332.7 978.7 %all-reduce.10.cloned.1.call-start = ((), (), s32[]{:S(2)}) async-start(), calls=%async_computation.1 | async-start | bytes 131072 | tf_op jit(solution)/shard_map/psum | solution.py:118
  (32 other events, 869.8 us)
Sparse Core Ops, SparseCore 0:
  331.5 75.1 all-reduce.7
  413.8 453.3 all-reduce.11
  870.1 441.2 all-reduce.9
